TPU v7x, 32 devices: a whole 2x2x4 slice. The times are simulated.
32 devices in a mesh: groups: 2 (over x), gy: 16 (over z, y, core).
Axes of the slice: x: 2, y: 2, z: 4, core: 2. Of those that a mesh axis runs over, the one named last changes fastest.
Arguments:
- state: float32 [8, 64, 128, 128], P(None, 'groups', 'gy'), parts along dimension 1
- base: float32 [8, 64, 128, 128], P(None, 'groups', 'gy'), parts along dimension 1
- shear_shift: int32 [64], P('groups'), parts along dimension 0, may hold values from 0 to 127
Outputs:
- advanced: float32 [8, 64, 128, 128], P(None, 'groups', 'gy'), parts along dimension 1
There are 2 independent parts, one for each index of `groups`. A program takes and returns all parts, laid end to end along the dimension named above; each array names one. Nothing has to cross between parts.
All inputs are finite; a program needn't handle non-finite values.
Results may differ from a plain program's by a relative error of at most 0.00002.
Values sent between devices are 32-bit elements; how exact they have to be, the bound alone decides.
A program may use at most 128 MiB of HBM per device.

v0:
```python
import jax
import jax.numpy as jnp
from jax import lax
from jax.sharding import PartitionSpec as P

GAMMA = 5.0 / 3.0
ADV = 0.1
DIFF = 0.1
DTIME = 0.2
OMEGA = 1.0
QSHEAR = 1.5
SHEAR_V = 0.75


def extended(array, sides, width):
    for axis, dim in sides:
        size, length = (lax.axis_size(axis), array.shape[dim])
        up = [(i, (i + 1) % size) for i in range(size)]
        down = [(j, i) for i, j in up]
        last = lax.slice_in_dim(array, length - width, length, axis=dim)
        first = lax.slice_in_dim(array, 0, width, axis=dim)
        before = lax.ppermute(last, axis, up)
        after = lax.ppermute(first, axis, down)
        array = jnp.concatenate([before, array, after], axis=dim)
    return array


def fluxes(fields, direction):
    density = fields[0]
    momenta = fields[1:4]
    magnet = fields[4:7]
    energy = fields[7]
    velocity = momenta / density
    magnet_sq = magnet[0] * magnet[0] + magnet[1] * magnet[1] + magnet[2] * magnet[2]
    kinetic = momenta[0] * velocity[0] + momenta[1] * velocity[1] + momenta[2] * velocity[2]
    total_p = (GAMMA - 1.0) * (energy - 0.5 * kinetic - 0.5 * magnet_sq) + 0.5 * magnet_sq
    cross_vb = velocity[0] * magnet[0] + velocity[1] * magnet[1] + velocity[2] * magnet[2]
    along_v = velocity[direction]
    along_b = magnet[direction]
    mom_flux = momenta * along_v - magnet * along_b
    mom_flux = mom_flux.at[direction].add(total_p)
    mag_flux = along_v * magnet - along_b * velocity
    energy_flux = (energy + total_p) * along_v - along_b * cross_vb
    return jnp.concatenate(
        [momenta[direction][None], mom_flux, mag_flux, energy_flux[None]], axis=0
    )


def sources(fields, xcoord):
    density = fields[0]
    mom_x = fields[1]
    mom_y = fields[2]
    tidal = 2.0 * QSHEAR * OMEGA * OMEGA * xcoord
    force_x = 2.0 * OMEGA * mom_y + tidal * density
    force_y = -2.0 * OMEGA * mom_x
    heating = tidal * mom_x
    zeros = jnp.zeros_like(density)
    return jnp.stack([zeros, force_x, force_y, zeros, zeros, zeros, zeros, heating])


def advance(state, base, lo_ghost, hi_ghost, y_hi, y_lo, fy_hi, fy_lo):
    width = state.shape[3]
    xcoord = (jnp.arange(width).astype(jnp.float32) + 0.5) / width - 0.5
    flux_x = fluxes(state, 0)
    x_hi = jnp.concatenate([state[..., 1:], hi_ghost], axis=3)
    x_lo = jnp.concatenate([lo_ghost, state[..., :-1]], axis=3)
    fx_hi = jnp.concatenate([flux_x[..., 1:], fluxes(hi_ghost, 0)], axis=3)
    fx_lo = jnp.concatenate([fluxes(lo_ghost, 0), flux_x[..., :-1]], axis=3)
    flux_z = fluxes(state, 2)
    fz_hi = jnp.roll(flux_z, -1, 1)
    fz_lo = jnp.roll(flux_z, 1, 1)
    z_hi = jnp.roll(state, -1, 1)
    z_lo = jnp.roll(state, 1, 1)
    diverge = fx_hi - fx_lo + (fy_hi - fy_lo) + (fz_hi - fz_lo)
    spread = x_hi + x_lo - 2.0 * state + (y_hi + y_lo - 2.0 * state) + (z_hi + z_lo - 2.0 * state)
    moved = state - ADV * diverge + DIFF * spread + DTIME * sources(state, xcoord)
    return 0.5 * base + 0.5 * moved


def on_device(state, base, shear_shift):
    rows_here = state.shape[2]
    cycle_size = lax.axis_size("gy")
    total_rows = rows_here * cycle_size
    first_row = lax.axis_index("gy") * rows_here
    edges = jnp.stack([state[:, :, :, -1], state[:, :, :, 0]])
    offsets = jnp.stack([shear_shift % total_rows, (total_rows - shear_shift) % total_rows])
    local_rows = jnp.arange(rows_here)
    whole = lax.all_gather(edges, "gy", axis=3, tiled=True)
    source = (first_row + local_rows[None, None, :] - offsets[:, :, None]) % total_rows
    ghosts = jnp.take_along_axis(whole, source[:, None], axis=3)
    lo_ghost = ghosts[0]
    hi_ghost = ghosts[1]
    lo_ghost = lo_ghost.at[2].add(SHEAR_V * lo_ghost[0])
    hi_ghost = hi_ghost.at[2].add(-SHEAR_V * hi_ghost[0])
    padded = extended(state, (("gy", 2),), 1)
    flux_pad = fluxes(padded, 1)
    return advance(
        state,
        base,
        lo_ghost[..., None],
        hi_ghost[..., None],
        padded[:, :, 2:],
        padded[:, :, :-2],
        flux_pad[:, :, 2:],
        flux_pad[:, :, :-2],
    )


def solution(mesh):
    return jax.shard_map(
        on_device,
        mesh=mesh,
        in_specs=(P(None, "groups", "gy", None), P(None, "groups", "gy", None), P("groups")),
        out_specs=P(None, "groups", "gy", None),
        check_vma=False,
    )
```

profile of v0, /device:TPU:23, one launch (start us, length us, event | category | flops | bytes accessed | tf_op | source)
XLA Modules:
  0.0 103.6 jit_solution(6912898926164120790)
XLA Ops:
  0.0 2.4 %fusion.69 = (f32[8,32,1,128]{3,2,1,0:T(1,128)}, f32[8,32,1,128]{3,2,1,0:T(1,128)}) fusion(f32[8,32,8,128]{3,2,1,0:T(8,128)} %param.17), kind=kLoop, calls=%fused_computation.170 | loop fusion | bytes 524288 | tf_op jit(solution)/shard_map/slice | solution.py:21
  2.4 1.8 %collective-permute-start = (f32[8,32,1,128]{3,1,2,0:T(8,128)}, f32[8,32,1,128]{3,1,2,0:T(8,128)}, u32[]{:S(2)}, u32[]{:S(2)}) collective-permute-start(f32[8,32,1,128]{3,1,2,0:T(8,128)} %bitcast.42), channel_id=1, source_target_pairs={{0,1},{1,2},{2,3},{3,4},{4,5},{5,6},{6,7},{7,8},{8,9},{9,10},{10,1... | collective-permute-start | bytes 393224 | tf_op jit(solution)/shard_map/ppermute | solution.py:22
  4.3 0.7 fusion.56
  5.1 0.7 broadcast_dynamic-update-slice_fusion.1
  5.8 3.0 %fusion.64 = (f32[8,31,8,128]{3,2,1,0:T(8,128)}, f32[8,31,8,128]{3,2,1,0:T(8,128)}) fusion(f32[8,32,8,128]{3,2,1,0:T(8,128)} %param.17), kind=kLoop, calls=%fused_computation.165 | loop fusion | bytes 4063232 | tf_op jit(solution)/shard_map/jit(_roll_static)/slice | solution.py:73
  9.2 1.7 %fusion.65 = (f32[8,32,8,127]{3,2,1,0:T(8,128)}, f32[8,32,8,127]{3,2,1,0:T(8,128)}) fusion(f32[8,32,8,128]{3,2,1,0:T(8,128)S(1)} %copy-done), kind=kLoop, calls=%fused_computation.166 | loop fusion | bytes 4161536 | tf_op jit(solution)/shard_map/slice | solution.py:66
  11.0 0.5 copy.73
  11.4 0.5 copy.74
  12.1 56.6 %all_gather.3 = f32[2,8,32,128]{1,3,2,0:T(8,128)} all-gather(f32[2,8,32,8]{1,3,2,0:T(8,128)S(1)} %copy.46), channel_id=1, replica_groups=mesh['groups'=2,'gy'=16] {'gy'}, dimensions={3}, use_global_device_ids=true | all-gather | bytes 278528 | tf_op jit(solution)/shard_map/all_gather | solution.py:88
  68.6 4.6 %gather_fusion = f32[512,8]{1,0:T(8,128)S(1)} fusion(f32[2,8,32,128]{1,3,2,0:T(8,128)} %all_gather.3, s32[512]{0:T(512)S(1)} %reshape.582), kind=kCustom, calls=%fused_computation | custom fusion | bytes 38912 | tf_op jit(solution)/shard_map/jit(take_along_axis)/gather | solution.py:90
  73.4 0.6 slice_bitcast_fusion.12
  74.0 0.5 copy.69
  74.5 0.6 slice_bitcast_fusion.11
  75.1 0.5 copy.70
  75.6 0.7 add_dynamic-update-slice_fusion
  76.2 0.7 multiply_dynamic-update-slice_fusion.1
  76.9 0.8 broadcast_dynamic-update-slice_fusion
  78.3 0.8 multiply_dynamic-update-slice_fusion
  79.3 0.4 copy-done.14
  79.7 1.7 %fusion.67 = (f32[8,32,8,127]{3,2,1,0:T(8,128)}, f32[8,32,8,127]{3,2,1,0:T(8,128)}) fusion(f32[8,32,8,128]{3,2,1,0:T(8,128)S(1)} %get-tuple-element.148), kind=kLoop, calls=%fused_computation.168 | loop fusion | bytes 4161536 | tf_op jit(solution)/shard_map/slice | solution.py:68
  81.4 1.4 %fusion.66 = (f32[8,31,8,128]{3,2,1,0:T(8,128)}, f32[8,31,8,128]{3,2,1,0:T(8,128)}) fusion(f32[8,32,8,128]{3,2,1,0:T(8,128)S(1)} %get-tuple-element.149), kind=kLoop, calls=%fused_computation.167 | loop fusion | bytes 4063232 | tf_op jit(solution)/shard_map/jit(_roll_static)/slice | solution.py:71
  82.9 1.3 %multiply_subtract_fusion.10 = (f32[3,32,8,1]{1,2,0,3:T(8,128)}, f32[3,32,8,1]{1,2,0,3:T(8,128)S(1)}) fusion(f32[8,32,8,1]{1,2,0,3:T(8,128)S(1)} %copy-done.22, f32[32,8]{0,1:T(8,128)S(1)} %copy-done.26, f32[32,8]{0,1:T(8,128)S(1)} %slice_bitcast_fusion.14, f32[32,8]{0,1:T(8,128)} %copy-done.24), kind=kLoop, calls=%fused_computation.97 | loop fusion | flops 5376 | bytes 15360 | tf_op jit(solution)/shard_map/sub | solution.py:42
  84.2 1.3 %fusion.39 = (f32[3,32,8,1]{1,2,0,3:T(8,128)S(1)}, f32[1,32,8,1]{1,2,3,0:T(8,128)S(1)}, f32[1,32,8,1]{1,2,0,3:T(8,128)}) fusion(f32[3,32,8,1]{1,2,0,3:T(8,128)S(1)} %get-tuple-element.136, f32[8,32,8,1]{1,2,3,0:T(8,128)S(1)} %bitcast.127, f32[8,32,8,1]{1,2,0,3:T(8,128)S(1)} %copy-done.22, f32[3,32,8,1]{1,2,0,3:T(8,128)S(1)} %slice_divide_fusion.2, ...), kind=kLoop, calls=%fused_computation.117 | loop fusion | flops 4864 | bytes 52224 | tf_op jit(solution)/shard_map/scatter-add | solution.py:41
  85.4 0.6 fusion.53
  86.1 0.7 fusion.47
  86.8 0.6 pad_maximum_fusion.13
  87.4 2.2 %copy.49 = f32[8,32,8,1]{3,2,1,0:T(8,128)} copy(f32[8,32,8,1]{1,2,3,0:T(8,128)} %pad_maximum_fusion.13) | data formatting | bytes 16384 | tf_op jit(solution)/shard_map/concatenate | solution.py:44
  89.6 1.3 %pad_maximum_fusion.14 = f32[8,32,8,1]{1,2,0,3:T(8,128)} fusion(f32[1,32,8,1]{1,2,0,3:T(8,128)} %fusion.53, f32[3,32,8,1]{1,2,0,3:T(8,128)} %get-tuple-element.135, f32[3,32,8,1]{1,2,0,3:T(8,128)S(1)} %get-tuple-element.89, f32[1,32,8,1]{1,2,0,3:T(8,128)} %get-tuple-element.139), kind=kLoop, calls=%fused_computation.92 | loop fusion | flops 6144 | bytes 16384 | tf_op jit(solution)/shard_map/concatenate | solution.py:44
  90.9 2.2 %copy.64 = f32[8,32,8,1]{3,2,1,0:T(8,128)} copy(f32[8,32,8,1]{1,2,0,3:T(8,128)} %pad_maximum_fusion.14) | data formatting | bytes 16384 | tf_op jit(solution)/shard_map/concatenate | solution.py:44
  93.1 1.3 %pad_maximum_fusion = f32[8,32,10,128]{3,2,1,0:T(8,128)S(1)} fusion(f32[8,32,1,128]{3,2,1,0:T(1,128)} %bitcast.34, f32[8,32,8,128]{3,2,1,0:T(8,128)S(1)} %copy-done, f32[8,32,1,128]{3,2,1,0:T(1,128)} %bitcast.33), kind=kLoop, calls=%fused_computation.1 | loop fusion | flops 655360 | bytes 2621440 | tf_op jit(solution)/shard_map/concatenate | solution.py:24
  97.5 0.4 copy-done.5
  99.5 4.0 %fusion.8 = f32[8,32,8,128]{3,2,1,0:T(8,128)} fusion(f32[8,32,8,128]{3,2,1,0:T(8,128)S(1)} %copy-done.18, f32[8,32,8,128]{3,2,1,0:T(8,128)S(1)} %copy-done, f32[8,32,1,128]{3,2,1,0:T(1,128)} %bitcast.33, f32[8,32,1,128]{3,2,1,0:T(1,128)} %bitcast.34, f32[1,32,8,128]{3,2,1,0:T(8,128)S(1)} %copy-done.15, f32[3,32,8,128]{3,2,1,0:T(8,128)S(1)} %copy-done.12, ...), kind=kLoop, calls=%fused_computation.12 | loop fusion | flops 9961472 | bytes 15925248 | tf_op jit(solution)/shard_map/add | solution.py:77
  (89 shorter events, 6.3 us)
Async XLA Ops:
  2.4 90.7 %collective-permute-start = (f32[8,32,1,128]{3,1,2,0:T(8,128)}, f32[8,32,1,128]{3,1,2,0:T(8,128)}, u32[]{:S(2)}, u32[]{:S(2)}) collective-permute-start(f32[8,32,1,128]{3,1,2,0:T(8,128)} %bitcast.42), channel_id=1, source_target_pairs={{0,1},{1,2},{2,3},{3,4},{4,5},{5,6},{6,7},{7,8},{8,9},{9,10},{10,1... | collective-permute-start | bytes 393224 | tf_op jit(solution)/shard_map/ppermute | solution.py:22
  4.2 88.9 %collective-permute-start.1 = (f32[8,32,1,128]{3,1,2,0:T(8,128)}, f32[8,32,1,128]{3,1,2,0:T(8,128)}, u32[]{:S(2)}, u32[]{:S(2)}) collective-permute-start(f32[8,32,1,128]{3,1,2,0:T(8,128)} %bitcast.43), channel_id=1, source_target_pairs={{1,0},{2,1},{3,2},{4,3},{5,4},{6,5},{7,6},{8,7},{9,8},{10,9},{11,1... | collective-permute-start | bytes 393224 | tf_op jit(solution)/shard_map/ppermute | solution.py:23
  5.1 3.7 %copy-start = (f32[8,32,8,128]{3,2,1,0:T(8,128)S(1)}, f32[8,32,8,128]{3,2,1,0:T(8,128)}, u32[]{:S(2)}) copy-start(f32[8,32,8,128]{3,2,1,0:T(8,128)} %param.17) | copy-start | bytes 3145732
  73.3 1.1 %copy-start.23 = (f32[2,8,32,8]{2,3,1,0:T(8,128)}, f32[2,8,32,8]{2,3,1,0:T(8,128)S(1)}, u32[]{:S(2)}) copy-start(f32[2,8,32,8]{2,3,1,0:T(8,128)S(1)} %select_bitcast_fusion) | copy-start | bytes 49156
  73.4 1.1 %copy-start.19 = (f32[8,32,8,1]{1,2,3,0:T(8,128)}, f32[8,32,8,1]{1,2,3,0:T(8,128)S(1)}, u32[]{:S(2)}) copy-start(f32[8,32,8,1]{1,2,3,0:T(8,128)S(1)} %constant_dynamic-update-slice_fusion) | copy-start | bytes 24580
  74.5 3.3 %copy-start.21 = (f32[8,32,8,1]{1,2,0,3:T(8,128)}, f32[8,32,8,1]{1,2,0,3:T(8,128)S(1)}, u32[]{:S(2)}) copy-start(f32[8,32,8,1]{1,2,0,3:T(8,128)S(1)} %bitcast_dynamic-update-slice_fusion) | copy-start | bytes 24580
  75.1 7.8 %copy-start.24 = (f32[32,8]{0,1:T(8,128)}, f32[32,8]{0,1:T(8,128)S(1)}, u32[]{:S(2)}) copy-start(f32[32,8]{0,1:T(8,128)S(1)} %get-tuple-element.140) | copy-start | bytes 3076
  78.1 1.0 copy-start.11
  79.1 0.6 copy-start.14
  79.1 0.7 copy-start.16
  81.4 1.4 %copy-start.22 = (f32[8,32,8,1]{1,2,0,3:T(8,128)S(1)}, f32[8,32,8,1]{1,2,0,3:T(8,128)}, u32[]{:S(2)}) copy-start(f32[8,32,8,1]{1,2,0,3:T(8,128)} %copy-done.21) | copy-start | bytes 24580
  81.4 1.5 %copy-start.26 = (f32[32,8]{0,1:T(8,128)S(1)}, f32[32,8]{0,1:T(8,128)}, u32[]{:S(2)}) copy-start(f32[32,8]{0,1:T(8,128)} %get-tuple-element.141) | copy-start | bytes 3076
  81.4 4.6 %copy-start.20 = (f32[8,32,8,1]{1,2,3,0:T(8,128)S(1)}, f32[8,32,8,1]{1,2,3,0:T(8,128)}, u32[]{:S(2)}) copy-start(f32[8,32,8,1]{1,2,3,0:T(8,128)} %copy-done.19) | copy-start | bytes 24580
  81.4 4.6 %copy-start.25 = (f32[32,8]{0,1:T(8,128)S(1)}, f32[32,8]{0,1:T(8,128)}, u32[]{:S(2)}) copy-start(f32[32,8]{0,1:T(8,128)} %get-tuple-element.145) | copy-start | bytes 3076
  94.6 1.2 %copy-start.10 = (f32[8,31,8,128]{3,2,1,0:T(8,128)S(1)}, f32[8,31,8,128]{3,2,1,0:T(8,128)}, u32[]{:S(2)}) copy-start(f32[8,31,8,128]{3,2,1,0:T(8,128)} %get-tuple-element.123) | copy-start | bytes 3047428
  94.6 1.5 %copy-start.13 = (f32[8,32,8,128]{3,2,1,0:T(8,128)S(1)}, f32[8,32,8,128]{3,2,1,0:T(8,128)}, u32[]{:S(2)}) copy-start(f32[8,32,8,128]{3,2,1,0:T(8,128)} %get-tuple-element.108) | copy-start | bytes 3145732
  94.6 1.8 %copy-start.18 = (f32[8,32,8,128]{3,2,1,0:T(8,128)S(1)}, f32[8,32,8,128]{3,2,1,0:T(8,128)}, u32[]{:S(2)}) copy-start(f32[8,32,8,128]{3,2,1,0:T(8,128)} %param.18) | copy-start | bytes 3145732
  94.8 2.0 %copy-start.7 = (f32[8,31,8,128]{3,2,1,0:T(8,128)S(1)}, f32[8,31,8,128]{3,2,1,0:T(8,128)}, u32[]{:S(2)}) copy-start(f32[8,31,8,128]{3,2,1,0:T(8,128)} %get-tuple-element.118) | copy-start | bytes 3047428
  94.9 2.3 %copy-start.8 = (f32[8,31,8,128]{3,2,1,0:T(8,128)S(1)}, f32[8,31,8,128]{3,2,1,0:T(8,128)}, u32[]{:S(2)}) copy-start(f32[8,31,8,128]{3,2,1,0:T(8,128)} %get-tuple-element.119) | copy-start | bytes 3047428
  94.9 2.6 %copy-start.9 = (f32[8,31,8,128]{3,2,1,0:T(8,128)S(1)}, f32[8,31,8,128]{3,2,1,0:T(8,128)}, u32[]{:S(2)}) copy-start(f32[8,31,8,128]{3,2,1,0:T(8,128)} %get-tuple-element.122) | copy-start | bytes 3047428
  94.9 2.6 %copy-start.12 = (f32[3,32,8,128]{3,2,1,0:T(8,128)S(1)}, f32[3,32,8,128]{3,2,1,0:T(8,128)}, u32[]{:S(2)}) copy-start(f32[3,32,8,128]{3,2,1,0:T(8,128)} %copy-done.11) | copy-start | bytes 1179652
  95.2 2.8 %copy-start.5 = (f32[8,32,8,127]{3,2,1,0:T(8,128)S(1)}, f32[8,32,8,127]{3,2,1,0:T(8,128)}, u32[]{:S(2)}) copy-start(f32[8,32,8,127]{3,2,1,0:T(8,128)} %get-tuple-element.124) | copy-start | bytes 3121156
  95.2 3.1 %copy-start.6 = (f32[8,32,8,127]{3,2,1,0:T(8,128)S(1)}, f32[8,32,8,127]{3,2,1,0:T(8,128)}, u32[]{:S(2)}) copy-start(f32[8,32,8,127]{3,2,1,0:T(8,128)} %get-tuple-element.125) | copy-start | bytes 3121156
  95.2 3.0 %copy-start.15 = (f32[1,32,8,128]{3,2,1,0:T(8,128)S(1)}, f32[1,32,8,128]{3,2,1,0:T(8,128)}, u32[]{:S(2)}) copy-start(f32[1,32,8,128]{3,2,1,0:T(8,128)} %copy-done.14) | copy-start | bytes 393220
  95.2 3.0 %copy-start.17 = (f32[1,32,8,128]{3,2,1,0:T(8,128)S(1)}, f32[1,32,8,128]{3,2,1,0:T(8,128)}, u32[]{:S(2)}) copy-start(f32[1,32,8,128]{3,2,1,0:T(8,128)} %copy-done.16) | copy-start | bytes 393220
  95.3 3.3 %copy-start.1 = (f32[8,32,8,1]{3,2,1,0:T(8,128)S(1)}, f32[8,32,8,1]{3,2,1,0:T(8,128)}, u32[]{:S(2)}) copy-start(f32[8,32,8,1]{3,2,1,0:T(8,128)} %copy.49) | copy-start | bytes 24580
  95.3 3.6 %copy-start.2 = (f32[8,32,8,1]{3,2,1,0:T(8,128)S(1)}, f32[8,32,8,1]{3,2,1,0:T(8,128)}, u32[]{:S(2)}) copy-start(f32[8,32,8,1]{3,2,1,0:T(8,128)} %copy.64) | copy-start | bytes 24580
  95.4 3.9 %copy-start.3 = (f32[8,32,8,127]{3,2,1,0:T(8,128)S(1)}, f32[8,32,8,127]{3,2,1,0:T(8,128)}, u32[]{:S(2)}) copy-start(f32[8,32,8,127]{3,2,1,0:T(8,128)} %get-tuple-element.120) | copy-start | bytes 3121156
  95.4 4.2 %copy-start.4 = (f32[8,32,8,127]{3,2,1,0:T(8,128)S(1)}, f32[8,32,8,127]{3,2,1,0:T(8,128)}, u32[]{:S(2)}) copy-start(f32[8,32,8,127]{3,2,1,0:T(8,128)} %get-tuple-element.121) | copy-start | bytes 3121156
where the time goes:
time: 104 us
  blocking collectives  56.6 us (54%)
  local copies, waits for them, and re-layouts  29.1 us (28%)
  other arithmetic  15.8 us (15%)
  starting transfers between devices  1.8 us (2%)
    all_gather x1, blocking collectives, on_device(): whole = lax.all_gather(edges, 'gy', axis=3, tiled=True)  56.6 us
    unnamed x58, local copies, waits for them, and re-layouts  6.96 us
    gather x3, local copies, waits for them, and re-layouts, on_device(): ghosts = jnp.take_along_axis(whole, source[:, None], axis=3)  4.78 us
    concatenate x2, local copies, waits for them, and re-layouts, fluxes(): jnp.concatenate([momenta[direction][None], mom_flux, mag_flux, energy_flu...  4.35 us
    add x1, other arithmetic, advance(): return 0.5 * base + 0.5 * moved  4.05 us
    slice x2, local copies, waits for them, and re-layouts, advance(): z_lo = jnp.roll(state, 1, 1)  3.03 us
    slice x1, local copies, waits for them, and re-layouts, extended(): first = lax.slice_in_dim(array, 0, width, axis=dim)  2.44 us
    scatter-add x4, other arithmetic, fluxes(): mom_flux = mom_flux.at[direction].add(total_p)  2.39 us
  transfers between devices with their start and end apart: 2, of which 0 were waited for; matrix products, arithmetic and copies ran while one was open for 30% of the time, Pallas kernels for 0%

commit v1 on v0

v1 whole, which is shorter than its diff:
```python
import functools

import jax
import jax.numpy as jnp
from jax import lax
from jax.experimental import pallas as pl
from jax.experimental.pallas import tpu as pltpu
from jax.sharding import PartitionSpec as P

SHEAR_V = 0.75
SCALE = 0.05
LANES = 128
ROWS = 8
MESH = pl.DeviceIdType.MESH


def products(u):
    inv = 1.0 / u[0]
    w = [u[1] * inv, u[2] * inv, u[3] * inv]
    b = [u[4], u[5], u[6]]
    c = [SCALE * f for f in u]
    mc, bc = c[1:4], c[4:7]
    kin = mc[0] * w[0] + mc[1] * w[1] + mc[2] * w[2]
    bsq = bc[0] * b[0] + bc[1] * b[1] + bc[2] * b[2]
    press = (2.0 / 3.0) * (c[7] - 0.5 * kin - 0.5 * bsq) + 0.5 * bsq
    cross = w[0] * b[0] + w[1] * b[1] + w[2] * b[2]
    return c, w, b, press, cross


def tensor(c, w, b, i, j):
    return c[1 + i] * w[j] - c[4 + i] * b[j]


def twist(c, w, i, j):
    return w[i] * c[4 + j] - c[4 + i] * w[j]


def energy_flux(c, w, press, cross, d):
    return (c[7] + press) * w[d] - c[4 + d] * cross


def flux_along(u, d):
    c, w, b, press, cross = products(u)
    out = [c[1 + d]]
    for i in range(3):
        t = tensor(c, w, b, i, d)
        out.append(t + press if i == d else t)
    for i in range(3):
        out.append(None if i == d else twist(c, w, d, i))
    out.append(energy_flux(c, w, press, cross, d))
    return c, out


def plus(a, f):
    return a if f is None else a + f


def minus(a, f):
    return a if f is None else a - f


def kernel(
    n, planes, shift_ref, state_hbm, base_hbm, out_hbm,
    st, bs, ov, gath, halo_out, halo_in,
    local_sem, halo_send, halo_recv, edge_send, edge_recv,
):
    me = lax.axis_index("gy")
    field = planes * ROWS
    right = lax.rem(me + 1, n)
    left = lax.rem(me + n - 1, n)

    load_state = pltpu.make_async_copy(state_hbm, st, local_sem.at[0])
    load_state.start()
    load_base = pltpu.make_async_copy(base_hbm, bs, local_sem.at[1])
    load_base.start()

    barrier = pltpu.get_barrier_semaphore()

    def greet(d, carry):
        pl.semaphore_signal(
            barrier, inc=1, device_id={"gy": lax.rem(me + d, n)}, device_id_type=MESH
        )
        return carry

    lax.fori_loop(1, n, greet, 0)

    lane = lax.broadcasted_iota(jnp.int32, (ROWS, LANES), 1)
    row = lax.broadcasted_iota(jnp.int32, (ROWS, LANES), 0)
    pair = lane // 2
    even = lane % 2 == 0

    load_state.wait()

    for f in range(8):
        for g in range(planes // ROWS):
            at = f * field + g * ROWS * ROWS
            to = pl.ds(f * planes + g * ROWS, ROWS)
            halo_out[0, to, :] = st[pl.ds(at, ROWS, stride=ROWS), :]
            halo_out[1, to, :] = st[pl.ds(at + ROWS - 1, ROWS, stride=ROWS), :]

    def plane_at(f, k):
        return pl.ds(pl.multiple_of(f * field + k * ROWS, ROWS), ROWS)

    def collect(k, acc):
        out = []
        for j in range(4):
            low = pltpu.roll(st[plane_at(j, k), :], 2 * k + 1, 1)
            high = pltpu.roll(st[plane_at(j + 4, k), :], 2 * k + 1 + 64, 1)
            keep = jnp.where(pair == k, low, acc[j])
            out.append(jnp.where(pair == k + 32, high, keep))
        return tuple(out)

    zero = jnp.zeros((ROWS, LANES), jnp.float32)
    edges = lax.fori_loop(0, planes, collect, (zero,) * 4, unroll=4)
    for j in range(4):
        gath[0, pl.ds(j * ROWS, ROWS), :] = edges[j]

    pl.semaphore_wait(barrier, n - 1)

    def edge_copy(d):
        return pltpu.make_async_remote_copy(
            src_ref=gath.at[0],
            dst_ref=gath.at[d],
            send_sem=edge_send.at[d],
            recv_sem=edge_recv.at[d],
            device_id={"gy": lax.rem(me + d, n)},
            device_id_type=MESH,
        )

    def halo_copy(s, target):
        return pltpu.make_async_remote_copy(
            src_ref=halo_out.at[s],
            dst_ref=halo_in.at[s],
            send_sem=halo_send.at[s],
            recv_sem=halo_recv.at[s],
            device_id={"gy": target},
            device_id_type=MESH,
        )

    def send_edge(d, carry):
        edge_copy(d).start()
        return carry

    lax.fori_loop(1, n, send_edge, 0)
    halos = [halo_copy(0, left), halo_copy(1, right)]
    for copy in halos:
        copy.start()

    load_base.wait()

    tidal = ((lane.astype(jnp.float32) + 0.5) / LANES - 0.5) * 6.0
    first_x, last_x = lane == 0, lane == LANES - 1
    first_y, last_y = row == 0, row == ROWS - 1

    def from_next_x(a):
        return jnp.where(last_x, 0.0, pltpu.roll(a, LANES - 1, 1))

    def from_prev_x(a):
        return jnp.where(first_x, 0.0, pltpu.roll(a, 1, 1))

    def from_next_y(a):
        return jnp.where(last_y, 0.0, pltpu.roll(a, ROWS - 1, 0))

    def from_prev_y(a):
        return jnp.where(first_y, 0.0, pltpu.roll(a, 1, 0))

    def plane_terms(u):
        c, w, b, press, cross = products(u)
        t = {(i, j): tensor(c, w, b, i, j) for i in range(3) for j in range(i, 3)}
        for i in range(3):
            t[i, i] = t[i, i] + press
        s = {(i, j): twist(c, w, i, j) for i in range(3) for j in range(i + 1, 3)}
        ahead, behind = [], []
        for d in range(3):
            fl = [c[1 + d]] + [t[min(i, d), max(i, d)] for i in range(3)]
            up = [c[f] + fl[f] for f in range(4)]
            down = [c[f] - fl[f] for f in range(4)]
            for i in range(3):
                a = c[4 + i]
                if i == d:
                    up.append(a)
                    down.append(a)
                elif d < i:
                    up.append(a + s[d, i])
                    down.append(a - s[d, i])
                else:
                    up.append(a - s[i, d])
                    down.append(a + s[i, d])
            e = energy_flux(c, w, press, cross, d)
            up.append(c[7] + e)
            down.append(c[7] - e)
            behind.append(up)
            ahead.append(down)
        return c, ahead, behind

    def load_plane(k):
        return [st[plane_at(f, k), :] for f in range(8)]

    def step(k, carry):
        partial, below = carry
        c, ahead, behind = plane_terms(load_plane(k))
        prev = lax.rem(k + planes - 1, planes)
        source = [4.0 * f for f in c]
        source[1] = 4.0 * (c[1] + c[2]) + tidal * c[0]
        source[2] = 4.0 * (c[2] - c[1])
        source[7] = source[7] + tidal * c[1]
        fresh = []
        for f in range(8):
            ov[plane_at(f, prev), :] = partial[f] + ahead[2][f]
            here = 0.5 * bs[plane_at(f, k), :] + source[f]
            here = here + (from_next_x(ahead[0][f]) + from_prev_x(behind[0][f]))
            here = here + (from_next_y(ahead[1][f]) + from_prev_y(behind[1][f]))
            fresh.append(here + below[f])
        return tuple(fresh), tuple(behind[2])

    u = load_plane(planes - 1)
    c, fl = flux_along(u, 2)
    below = tuple(plus(c[f], fl[f]) for f in range(8))
    partial, _ = lax.fori_loop(0, planes, step, ((zero,) * 8, below), unroll=2)
    for f in range(8):
        at = plane_at(f, planes - 1)
        ov[at, :] = ov[at, :] + partial[f]

    for s, combine, to_row in ((0, minus, ROWS - 1), (1, plus, 0)):
        halos[s].wait_recv()
        for g in range(planes // ROWS):
            u = [halo_in[s, pl.ds(f * planes + g * ROWS, ROWS), :] for f in range(8)]
            c, fl = flux_along(u, 1)
            for f in range(8):
                at = pl.ds(f * field + g * ROWS * ROWS + to_row, ROWS, stride=ROWS)
                ov[at, :] = ov[at, :] + combine(c[f], fl[f])

    cells = n * ROWS
    shift = jnp.zeros((ROWS, LANES), jnp.int32)
    for k in range(planes):
        shift = jnp.where(pair % 32 == k, shift_ref[k], shift)
    shift = jnp.where(even, shift, jnp.where(shift == 0, 0, cells - shift))
    hop = shift // ROWS
    fine = shift % ROWS
    hop_next = jnp.where(hop == n - 1, 0, hop + 1)

    def pick(d, carry):
        near, far = carry
        tiles = [gath[d, pl.ds(j * ROWS, ROWS), :] for j in range(4)]
        is_near, is_far = hop == d, hop_next == d
        return (
            tuple(jnp.where(is_near, tiles[j], near[j]) for j in range(4)),
            tuple(jnp.where(is_far, tiles[j], far[j]) for j in range(4)),
        )

    def wait_pick(d, carry):
        edge_copy(d).wait_recv()
        return pick(d, carry)

    chosen = pick(0, ((zero,) * 4, (zero,) * 4))
    near, far = lax.fori_loop(1, n, wait_pick, chosen)

    ghost = [None] * 8
    for j in range(4):
        a, b = near[j], far[j]
        for bit in (4, 2, 1):
            ra, rb = pltpu.roll(a, bit, 0), pltpu.roll(b, bit, 0)
            take = (fine // bit) % 2 == 1
            a = jnp.where(take, jnp.where(row < bit, rb, ra), a)
            b = jnp.where(take, rb, b)
        ghost[j] = a
        ghost[j + 4] = pltpu.roll(a, 64, 1)
    sign = jnp.where(even, 1.0, -1.0)
    ghost[0] = jnp.where(lane < 2 * planes, ghost[0], 1.0)
    ghost[2] = ghost[2] + sign * (SHEAR_V * ghost[0])
    c, fl = flux_along(ghost, 0)
    side = []
    for f in range(8):
        e = c[f] if fl[f] is None else c[f] + sign * fl[f]
        side.append(jnp.where(even, pltpu.roll(e, LANES - 1, 1), pltpu.roll(e, 1, 1)))
    outer = jnp.logical_or(first_x, last_x)

    def put_edges(k, carry):
        for f in range(8):
            at = plane_at(f, k)
            add = pltpu.roll(side[f], LANES - 1 - 2 * k, 1)
            ov[at, :] = ov[at, :] + jnp.where(outer, add, 0.0)
        return carry

    lax.fori_loop(0, planes, put_edges, 0, unroll=4)

    store = pltpu.make_async_copy(ov, out_hbm, local_sem.at[2])
    store.start()
    for copy in halos:
        copy.wait_send()

    def wait_edge(d, carry):
        edge_copy(d).wait_send()
        return carry

    lax.fori_loop(1, n, wait_edge, 0)
    store.wait()


def on_device(n, state, base, shear_shift):
    shape = state.shape
    planes = shape[1]
    assert shape[0] == 8 and shape[2] == ROWS and shape[3] == LANES and planes == 32
    total = 8 * planes * ROWS
    out = pl.pallas_call(
        functools.partial(kernel, n, planes),
        out_shape=jax.ShapeDtypeStruct((total, LANES), jnp.float32),
        in_specs=[
            pl.BlockSpec(memory_space=pltpu.SMEM),
            pl.BlockSpec(memory_space=pl.ANY),
            pl.BlockSpec(memory_space=pl.ANY),
        ],
        out_specs=pl.BlockSpec(memory_space=pl.ANY),
        scratch_shapes=[
            pltpu.VMEM((total, LANES), jnp.float32),
            pltpu.VMEM((total, LANES), jnp.float32),
            pltpu.VMEM((total, LANES), jnp.float32),
            pltpu.VMEM((n, 4 * ROWS, LANES), jnp.float32),
            pltpu.VMEM((2, 8 * planes, LANES), jnp.float32),
            pltpu.VMEM((2, 8 * planes, LANES), jnp.float32),
            pltpu.SemaphoreType.DMA((3,)),
            pltpu.SemaphoreType.DMA((2,)),
            pltpu.SemaphoreType.DMA((2,)),
            pltpu.SemaphoreType.DMA((n,)),
            pltpu.SemaphoreType.DMA((n,)),
        ],
        compiler_params=pltpu.CompilerParams(
            collective_id=0, has_side_effects=True, vmem_limit_bytes=24 * 1024 * 1024
        ),
    )(shear_shift, state.reshape(total, LANES), base.reshape(total, LANES))
    return out.reshape(shape)


def solution(mesh):
    return jax.shard_map(
        functools.partial(on_device, mesh.shape["gy"]),
        mesh=mesh,
        in_specs=(P(None, "groups", "gy", None), P(None, "groups", "gy", None), P("groups")),
        out_specs=P(None, "groups", "gy", None),
        check_vma=False,
    )
```

time: 104 us -> 20.1 us (0.19)
  the two profiles are of different devices: /device:TPU:23 before, /device:TPU:0 now
where the time goes in v1:
time: 20.1 us; the launch traced here: 20 us
  Pallas kernels  15.9 us (79%)
  local copies, waits for them, and re-layouts  4.08 us (20%)
    pallas_call x1, Pallas kernels, on_device(): pl.pallas_call(functools.partial(kernel, n, planes), out_shape=jax.ShapeD...  15.9 us
    unnamed x7, local copies, waits for them, and re-layouts  4.08 us

profile of v1, /device:TPU:0, one launch (start us, length us, event | category | flops | bytes accessed | tf_op | source)
XLA Modules:
  0.0 20.0 jit_solution(2360893936827267853)
XLA Ops:
  0.0 0.0 copy-start.2
  0.0 0.7 %copy-done.2 = s32[32]{0:T(128)S(1)} copy-done((s32[32]{0:T(128)S(1)}, s32[32]{0:T(128)}, u32[]{:S(2)}) %copy-start.2) | copy-done | bytes 152
  0.7 0.0 copy-start
  0.7 1.2 %copy-done = f32[8,32,8,128]{3,2,1,0:T(8,128)S(1)} copy-done((f32[8,32,8,128]{3,2,1,0:T(8,128)S(1)}, f32[8,32,8,128]{3,2,1,0:T(8,128)}, u32[]{:S(2)}) %copy-start) | copy-done | bytes 1048600
  1.9 0.0 copy-start.1
  1.9 1.2 %copy-done.1 = f32[8,32,8,128]{3,2,1,0:T(8,128)S(1)} copy-done((f32[8,32,8,128]{3,2,1,0:T(8,128)S(1)}, f32[8,32,8,128]{3,2,1,0:T(8,128)}, u32[]{:S(2)}) %copy-start.1) | copy-done | bytes 1048600
  3.1 15.9 %shard_map.37 = f32[2048,128]{1,0:T(8,128)S(1)} custom-call(s32[32]{0:T(128)S(1)} %copy-done.2, f32[2048,128]{1,0:T(8,128)S(1)} %bitcast.4, f32[2048,128]{1,0:T(8,128)S(1)} %bitcast.5), custom_call_target="tpu_custom_call" | custom-call | tf_op jit(solution)/shard_map/pallas_call | solution.py:305
  19.0 1.0 %copy.5 = f32[8,32,8,128]{3,2,1,0:T(8,128)} copy(f32[8,32,8,128]{3,2,1,0:T(8,128)S(1)} %bitcast.3) | data formatting | bytes 2097152
Async XLA Ops:
  0.0 0.7 %copy-start.2 = (s32[32]{0:T(128)S(1)}, s32[32]{0:T(128)}, u32[]{:S(2)}) copy-start(s32[32]{0:T(128)} %shift_ref.1) | copy-start | bytes 388
  0.7 1.2 %copy-start = (f32[8,32,8,128]{3,2,1,0:T(8,128)S(1)}, f32[8,32,8,128]{3,2,1,0:T(8,128)}, u32[]{:S(2)}) copy-start(f32[8,32,8,128]{3,2,1,0:T(8,128)} %param.3) | copy-start | bytes 3145732
  1.9 1.2 %copy-start.1 = (f32[8,32,8,128]{3,2,1,0:T(8,128)S(1)}, f32[8,32,8,128]{3,2,1,0:T(8,128)}, u32[]{:S(2)}) copy-start(f32[8,32,8,128]{3,2,1,0:T(8,128)} %param.4) | copy-start | bytes 3145732

commit v2 on v1

--- a/solution.py
+++ b/solution.py
@@ -10,6 +10,7 @@
 SHEAR_V = 0.75
 SCALE = 0.05
 LANES = 128
+FIRST = 16
 ROWS = 8
 MESH = pl.DeviceIdType.MESH
 
@@ -60,11 +61,13 @@
 
 
 def kernel(
-    n, planes, shift_ref, state_hbm, base_hbm, out_hbm,
-    st, bs, ov, gath, halo_out, halo_in,
-    local_sem, halo_send, halo_recv, edge_send, edge_recv,
+    outer, inner, planes, shift_ref, state_hbm, base_hbm, ov,
+    st, bs, gath, relay, caught, halo_out, halo_in,
+    local_sem, halo_send, halo_recv, edge_send, edge_recv, relay_send, relay_recv,
 ):
+    n = outer * inner
     me = lax.axis_index("gy")
+    high, low = me // inner, lax.rem(me, inner)
     field = planes * ROWS
     right = lax.rem(me + 1, n)
     left = lax.rem(me + n - 1, n)
@@ -76,13 +79,13 @@
 
     barrier = pltpu.get_barrier_semaphore()
 
-    def greet(d, carry):
+    across = [lax.rem(me + a * inner, n) for a in range(1, outer)]
+    within = [high * inner + lax.rem(low + b, inner) for b in range(1, inner)]
+    partners = across + within + [left, right]
+    for partner in partners:
         pl.semaphore_signal(
-            barrier, inc=1, device_id={"gy": lax.rem(me + d, n)}, device_id_type=MESH
+            barrier, inc=1, device_id={"gy": partner}, device_id_type=MESH
         )
-        return carry
-
-    lax.fori_loop(1, n, greet, 0)
 
     lane = lax.broadcasted_iota(jnp.int32, (ROWS, LANES), 1)
     row = lax.broadcasted_iota(jnp.int32, (ROWS, LANES), 0)
@@ -115,7 +118,7 @@
     for j in range(4):
         gath[0, pl.ds(j * ROWS, ROWS), :] = edges[j]
 
-    pl.semaphore_wait(barrier, n - 1)
+    pl.semaphore_wait(barrier, len(partners))
 
     def edge_copy(d):
         return pltpu.make_async_remote_copy(
@@ -123,7 +126,17 @@
             dst_ref=gath.at[d],
             send_sem=edge_send.at[d],
             recv_sem=edge_recv.at[d],
-            device_id={"gy": lax.rem(me + d, n)},
+            device_id={"gy": across[d - 1]},
+            device_id_type=MESH,
+        )
+
+    def relay_copy(d):
+        return pltpu.make_async_remote_copy(
+            src_ref=relay.at[d],
+            dst_ref=caught.at[d],
+            send_sem=relay_send.at[d],
+            recv_sem=relay_recv.at[d],
+            device_id={"gy": within[d - 1]},
             device_id_type=MESH,
         )
 
@@ -137,11 +150,9 @@
             device_id_type=MESH,
         )
 
-    def send_edge(d, carry):
-        edge_copy(d).start()
-        return carry
-
-    lax.fori_loop(1, n, send_edge, 0)
+    edge_copies = [edge_copy(d) for d in range(1, outer)]
+    for copy in edge_copies:
+        copy.start()
     halos = [halo_copy(0, left), halo_copy(1, right)]
     for copy in halos:
         copy.start()
@@ -216,7 +227,42 @@
     u = load_plane(planes - 1)
     c, fl = flux_along(u, 2)
     below = tuple(plus(c[f], fl[f]) for f in range(8))
-    partial, _ = lax.fori_loop(0, planes, step, ((zero,) * 8, below), unroll=2)
+    carry = lax.fori_loop(0, FIRST, step, ((zero,) * 8, below), unroll=2)
+
+    cells = n * ROWS
+    shift = jnp.zeros((ROWS, LANES), jnp.int32)
+    for k in range(planes):
+        shift = jnp.where(pair % 32 == k, shift_ref[k], shift)
+    shift = jnp.where(even, shift, jnp.where(shift == 0, 0, cells - shift))
+    hop = shift // ROWS
+    fine = shift % ROWS
+    hop_next = jnp.where(hop == n - 1, 0, hop + 1)
+
+    def locate(hops, target):
+        over, rest = hops // inner, hops % inner
+        wraps = rest > target
+        over = jnp.where(wraps, over + 1, over)
+        column = target - rest + jnp.where(wraps, inner, 0)
+        return jnp.where(over == outer, 0, over), column
+
+    for copy in edge_copies:
+        copy.wait_recv()
+    for b in range(inner):
+        target = lax.rem(low + b, inner)
+        over, column = locate(hop, target)
+        over_next, _ = locate(hop_next, target)
+        slot = jnp.where(column == low, over, over_next)
+        for j in range(4):
+            part = pl.ds(j * ROWS, ROWS)
+            tile = gath[0, part, :]
+            for d in range(1, outer):
+                tile = jnp.where(slot == d, gath[d, part, :], tile)
+            (relay if b else caught)[b, part, :] = tile
+    relay_copies = [relay_copy(d) for d in range(1, inner)]
+    for copy in relay_copies:
+        copy.start()
+
+    partial, _ = lax.fori_loop(FIRST, planes, step, carry, unroll=2)
     for f in range(8):
         at = plane_at(f, planes - 1)
         ov[at, :] = ov[at, :] + partial[f]
@@ -230,30 +276,18 @@
                 at = pl.ds(f * field + g * ROWS * ROWS + to_row, ROWS, stride=ROWS)
                 ov[at, :] = ov[at, :] + combine(c[f], fl[f])
 
-    cells = n * ROWS
-    shift = jnp.zeros((ROWS, LANES), jnp.int32)
-    for k in range(planes):
-        shift = jnp.where(pair % 32 == k, shift_ref[k], shift)
-    shift = jnp.where(even, shift, jnp.where(shift == 0, 0, cells - shift))
-    hop = shift // ROWS
-    fine = shift % ROWS
-    hop_next = jnp.where(hop == n - 1, 0, hop + 1)
-
-    def pick(d, carry):
-        near, far = carry
-        tiles = [gath[d, pl.ds(j * ROWS, ROWS), :] for j in range(4)]
-        is_near, is_far = hop == d, hop_next == d
-        return (
-            tuple(jnp.where(is_near, tiles[j], near[j]) for j in range(4)),
-            tuple(jnp.where(is_far, tiles[j], far[j]) for j in range(4)),
-        )
-
-    def wait_pick(d, carry):
-        edge_copy(d).wait_recv()
-        return pick(d, carry)
-
-    chosen = pick(0, ((zero,) * 4, (zero,) * 4))
-    near, far = lax.fori_loop(1, n, wait_pick, chosen)
+    for copy in relay_copies:
+        copy.wait_recv()
+    near, far = [], []
+    for j in range(4):
+        part = pl.ds(j * ROWS, ROWS)
+        a = b = caught[0, part, :]
+        for d in range(1, inner):
+            tile = caught[d, part, :]
+            a = jnp.where(hop % inner == d, tile, a)
+            b = jnp.where(hop_next % inner == d, tile, b)
+        near.append(a)
+        far.append(b)
 
     ghost = [None] * 8
     for j in range(4):
@@ -273,28 +307,19 @@
     for f in range(8):
         e = c[f] if fl[f] is None else c[f] + sign * fl[f]
         side.append(jnp.where(even, pltpu.roll(e, LANES - 1, 1), pltpu.roll(e, 1, 1)))
-    outer = jnp.logical_or(first_x, last_x)
+    rim = jnp.logical_or(first_x, last_x)
 
     def put_edges(k, carry):
         for f in range(8):
             at = plane_at(f, k)
             add = pltpu.roll(side[f], LANES - 1 - 2 * k, 1)
-            ov[at, :] = ov[at, :] + jnp.where(outer, add, 0.0)
+            ov[at, :] = ov[at, :] + jnp.where(rim, add, 0.0)
         return carry
 
     lax.fori_loop(0, planes, put_edges, 0, unroll=4)
 
-    store = pltpu.make_async_copy(ov, out_hbm, local_sem.at[2])
-    store.start()
-    for copy in halos:
+    for copy in halos + edge_copies + relay_copies:
         copy.wait_send()
-
-    def wait_edge(d, carry):
-        edge_copy(d).wait_send()
-        return carry
-
-    lax.fori_loop(1, n, wait_edge, 0)
-    store.wait()
 
 
 def on_device(n, state, base, shear_shift):
@@ -302,30 +327,36 @@
     planes = shape[1]
     assert shape[0] == 8 and shape[2] == ROWS and shape[3] == LANES and planes == 32
     total = 8 * planes * ROWS
+    inner = 1 << ((n.bit_length() - 1) // 2)
+    outer = n // inner
+    assert outer * inner == n
     out = pl.pallas_call(
-        functools.partial(kernel, n, planes),
-        out_shape=jax.ShapeDtypeStruct((total, LANES), jnp.float32),
+        functools.partial(kernel, outer, inner, planes),
+        out_shape=pltpu.VMEM((total, LANES), jnp.float32),
         in_specs=[
             pl.BlockSpec(memory_space=pltpu.SMEM),
-            pl.BlockSpec(memory_space=pl.ANY),
-            pl.BlockSpec(memory_space=pl.ANY),
+            pl.BlockSpec(memory_space=pltpu.HBM),
+            pl.BlockSpec(memory_space=pltpu.HBM),
         ],
-        out_specs=pl.BlockSpec(memory_space=pl.ANY),
+        out_specs=pl.BlockSpec(memory_space=pltpu.VMEM),
         scratch_shapes=[
             pltpu.VMEM((total, LANES), jnp.float32),
             pltpu.VMEM((total, LANES), jnp.float32),
-            pltpu.VMEM((total, LANES), jnp.float32),
-            pltpu.VMEM((n, 4 * ROWS, LANES), jnp.float32),
+            pltpu.VMEM((outer, 4 * ROWS, LANES), jnp.float32),
+            pltpu.VMEM((inner, 4 * ROWS, LANES), jnp.float32),
+            pltpu.VMEM((inner, 4 * ROWS, LANES), jnp.float32),
             pltpu.VMEM((2, 8 * planes, LANES), jnp.float32),
             pltpu.VMEM((2, 8 * planes, LANES), jnp.float32),
-            pltpu.SemaphoreType.DMA((3,)),
             pltpu.SemaphoreType.DMA((2,)),
             pltpu.SemaphoreType.DMA((2,)),
-            pltpu.SemaphoreType.DMA((n,)),
-            pltpu.SemaphoreType.DMA((n,)),
+            pltpu.SemaphoreType.DMA((2,)),
+            pltpu.SemaphoreType.DMA((outer,)),
+            pltpu.SemaphoreType.DMA((outer,)),
+            pltpu.SemaphoreType.DMA((inner,)),
+            pltpu.SemaphoreType.DMA((inner,)),
         ],
         compiler_params=pltpu.CompilerParams(
-            collective_id=0, has_side_effects=True, vmem_limit_bytes=24 * 1024 * 1024
+            collective_id=0, has_side_effects=True, vmem_limit_bytes=64 * 1024 * 1024 - 1536 * 1024
         ),
     )(shear_shift, state.reshape(total, LANES), base.reshape(total, LANES))
     return out.reshape(shape)

time: 20.1 us -> 15.3 us (0.76)
  local copies, waits for them, and re-layouts: 4.08 us -> 0.97 us
  Pallas kernels: 15.9 us -> 14.1 us
    unnamed x7 -> x1, local copies, waits for them, and re-layouts: 4.08 us -> 0.97 us
    pallas_call x1, Pallas kernels: 15.9 us -> 14.1 us  [on_device(): pl.pallas_call(functools.partial(kernel, outer, inner, planes), out_shape...]
where the time goes in v2:
time: 15.3 us; the launch traced here: 15.1 us
  Pallas kernels  14.1 us (92%)
  local copies, waits for them, and re-layouts  0.97 us (6%)
    pallas_call x1, Pallas kernels, on_device(): pl.pallas_call(functools.partial(kernel, outer, inner, planes), out_shape...  14.1 us
    unnamed x1, local copies, waits for them, and re-layouts  0.97 us

profile of v2, /device:TPU:0, one launch (start us, length us, event | category | flops | bytes accessed | tf_op | source)
XLA Modules:
  0.0 15.1 jit_solution(17219713922734795239)
XLA Ops:
  0.0 14.1 %shard_map.37 = f32[2048,128]{1,0:T(8,128)S(1)} custom-call(s32[32]{0:T(128)} %shift_ref.1, f32[2048,128]{1,0:T(8,128)} %bitcast.4, f32[2048,128]{1,0:T(8,128)} %bitcast.5), custom_call_target="tpu_custom_call" | custom-call | tf_op jit(solution)/shard_map/pallas_call | solution.py:333
  14.2 1.0 %copy.5 = f32[8,32,8,128]{3,2,1,0:T(8,128)} copy(f32[8,32,8,128]{3,2,1,0:T(8,128)S(1)} %bitcast.3) | data formatting | bytes 2097152

commit v3 on v2

--- a/solution.py
+++ b/solution.py
@@ -61,7 +61,7 @@
 
 
 def kernel(
-    outer, inner, planes, shift_ref, state_hbm, base_hbm, ov,
+    outer, inner, planes, shift_ref, state_hbm, base_hbm, ov, side_ref,
     st, bs, gath, relay, caught, halo_out, halo_in,
     local_sem, halo_send, halo_recv, edge_send, edge_recv, relay_send, relay_recv,
 ):
@@ -307,19 +307,29 @@
     for f in range(8):
         e = c[f] if fl[f] is None else c[f] + sign * fl[f]
         side.append(jnp.where(even, pltpu.roll(e, LANES - 1, 1), pltpu.roll(e, 1, 1)))
-    rim = jnp.logical_or(first_x, last_x)
-
-    def put_edges(k, carry):
-        for f in range(8):
-            at = plane_at(f, k)
-            add = pltpu.roll(side[f], LANES - 1 - 2 * k, 1)
-            ov[at, :] = ov[at, :] + jnp.where(rim, add, 0.0)
-        return carry
-
-    lax.fori_loop(0, planes, put_edges, 0, unroll=4)
+    for f in range(8):
+        side_ref[pl.ds(f * ROWS, ROWS), :] = side[f]
 
     for copy in halos + edge_copies + relay_copies:
         copy.wait_send()
+
+
+def finish(planes, inside, side, out_hbm, done, sem):
+    lane = lax.broadcasted_iota(jnp.int32, (ROWS, LANES), 1)
+    rim = jnp.logical_or(lane == 0, lane == LANES - 1)
+    field = planes * ROWS
+    copies = []
+    for f in range(8):
+        edge = side[pl.ds(f * ROWS, ROWS), :]
+        for k in range(planes):
+            at = pl.ds(f * field + k * ROWS, ROWS)
+            add = pltpu.roll(edge, LANES - 1 - 2 * k, 1)
+            done[at, :] = inside[at, :] + jnp.where(rim, add, 0.0)
+        part = pl.ds(f * field, field)
+        copies.append(pltpu.make_async_copy(done.at[part], out_hbm.at[part], sem.at[f]))
+        copies[f].start()
+    for copy in copies:
+        copy.wait()
 
 
 def on_device(n, state, base, shear_shift):
@@ -330,15 +340,18 @@
     inner = 1 << ((n.bit_length() - 1) // 2)
     outer = n // inner
     assert outer * inner == n
-    out = pl.pallas_call(
+    inside, side = pl.pallas_call(
         functools.partial(kernel, outer, inner, planes),
-        out_shape=pltpu.VMEM((total, LANES), jnp.float32),
+        out_shape=(
+            pltpu.VMEM((total, LANES), jnp.float32),
+            pltpu.VMEM((8 * ROWS, LANES), jnp.float32),
+        ),
         in_specs=[
             pl.BlockSpec(memory_space=pltpu.SMEM),
             pl.BlockSpec(memory_space=pltpu.HBM),
             pl.BlockSpec(memory_space=pltpu.HBM),
         ],
-        out_specs=pl.BlockSpec(memory_space=pltpu.VMEM),
+        out_specs=[pl.BlockSpec(memory_space=pltpu.VMEM)] * 2,
         scratch_shapes=[
             pltpu.VMEM((total, LANES), jnp.float32),
             pltpu.VMEM((total, LANES), jnp.float32),
@@ -359,6 +372,17 @@
             collective_id=0, has_side_effects=True, vmem_limit_bytes=64 * 1024 * 1024 - 1536 * 1024
         ),
     )(shear_shift, state.reshape(total, LANES), base.reshape(total, LANES))
+    out = pl.pallas_call(
+        functools.partial(finish, planes),
+        out_shape=jax.ShapeDtypeStruct((total, LANES), jnp.float32),
+        in_specs=[pl.BlockSpec(memory_space=pltpu.VMEM)] * 2,
+        out_specs=pl.BlockSpec(memory_space=pltpu.HBM),
+        scratch_shapes=[
+            pltpu.VMEM((total, LANES), jnp.float32),
+            pltpu.SemaphoreType.DMA((8,)),
+        ],
+        compiler_params=pltpu.CompilerParams(vmem_limit_bytes=8 * 1024 * 1024),
+    )(inside, side)
     return out.reshape(shape)
 
 

time: 15.3 us -> 14.6 us (0.954)
  local copies, waits for them, and re-layouts: 0.97 us -> 0 us
  Pallas kernels: 14.1 us -> 14.5 us
    pallas_call x0 -> x1, Pallas kernels: none -> 1.13 us  [on_device(): pl.pallas_call(functools.partial(finish, planes), out_shape=jax.ShapeDtyp...]
    unnamed x1 -> x0, local copies, waits for them, and re-layouts: 0.97 us -> none
    pallas_call x1, Pallas kernels: 14.1 us -> 13.3 us  [on_device(): pl.pallas_call(functools.partial(kernel, outer, inner, planes), out_shape...]
where the time goes in v3:
time: 14.6 us; the launch traced here: 14.5 us
  Pallas kernels  14.5 us (99%)
    pallas_call x1, Pallas kernels, on_device(): pl.pallas_call(functools.partial(kernel, outer, inner, planes), out_shape...  13.3 us
    pallas_call x1, Pallas kernels, on_device(): pl.pallas_call(functools.partial(finish, planes), out_shape=jax.ShapeDtyp...  1.13 us

profile of v3, /device:TPU:0, one launch (start us, length us, event | category | flops | bytes accessed | tf_op | source)
XLA Modules:
  0.0 14.5 jit_solution(4547282770125489152)
XLA Ops:
  0.0 13.3 %shard_map.37 = (f32[2048,128]{1,0:T(8,128)S(1)}, f32[64,128]{1,0:T(8,128)S(1)}) custom-call(s32[32]{0:T(128)} %shift_ref.1, f32[2048,128]{1,0:T(8,128)} %bitcast.3, f32[2048,128]{1,0:T(8,128)} %bitcast.4), custom_call_target="tpu_custom_call" | custom-call | tf_op jit(solution)/shard_map/pallas_call | solution.py:343
  13.3 1.1 %shard_map.38 = f32[2048,128]{1,0:T(8,128)} custom-call(f32[2048,128]{1,0:T(8,128)S(1)} %get-tuple-element.7.inside, f32[64,128]{1,0:T(8,128)S(1)} %get-tuple-element.8.side), custom_call_target="tpu_custom_call" | custom-call | tf_op jit(solution)/shard_map/pallas_call | solution.py:375

commit v4 on v3

--- a/solution.py
+++ b/solution.py
@@ -267,15 +267,6 @@
         at = plane_at(f, planes - 1)
         ov[at, :] = ov[at, :] + partial[f]
 
-    for s, combine, to_row in ((0, minus, ROWS - 1), (1, plus, 0)):
-        halos[s].wait_recv()
-        for g in range(planes // ROWS):
-            u = [halo_in[s, pl.ds(f * planes + g * ROWS, ROWS), :] for f in range(8)]
-            c, fl = flux_along(u, 1)
-            for f in range(8):
-                at = pl.ds(f * field + g * ROWS * ROWS + to_row, ROWS, stride=ROWS)
-                ov[at, :] = ov[at, :] + combine(c[f], fl[f])
-
     for copy in relay_copies:
         copy.wait_recv()
     near, far = [], []
@@ -310,6 +301,15 @@
     for f in range(8):
         side_ref[pl.ds(f * ROWS, ROWS), :] = side[f]
 
+    for s, combine, to_row in ((0, minus, ROWS - 1), (1, plus, 0)):
+        halos[s].wait_recv()
+        for g in range(planes // ROWS):
+            u = [halo_in[s, pl.ds(f * planes + g * ROWS, ROWS), :] for f in range(8)]
+            c, fl = flux_along(u, 1)
+            for f in range(8):
+                at = pl.ds(f * field + g * ROWS * ROWS + to_row, ROWS, stride=ROWS)
+                ov[at, :] = ov[at, :] + combine(c[f], fl[f])
+
     for copy in halos + edge_copies + relay_copies:
         copy.wait_send()
 
@@ -337,7 +337,7 @@
     planes = shape[1]
     assert shape[0] == 8 and shape[2] == ROWS and shape[3] == LANES and planes == 32
     total = 8 * planes * ROWS
-    inner = 1 << ((n.bit_length() - 1) // 2)
+    inner = 2
     outer = n // inner
     assert outer * inner == n
     inside, side = pl.pallas_call(

time: 14.6 us -> 14.5 us (level)
  no operation moved by 1% of the time
where the time goes in v4:
time: 14.5 us; the launch traced here: 14.4 us
  Pallas kernels  14.4 us (99%)
    pallas_call x1, Pallas kernels, on_device(): pl.pallas_call(functools.partial(kernel, outer, inner, planes), out_shape...  13.3 us
    pallas_call x1, Pallas kernels, on_device(): pl.pallas_call(functools.partial(finish, planes), out_shape=jax.ShapeDtyp...  1.13 us

profile of v4, /device:TPU:0, one launch (start us, length us, event | category | flops | bytes accessed | tf_op | source)
XLA Modules:
  0.0 14.4 jit_solution(1004391768782113688)
XLA Ops:
  0.0 13.3 %shard_map.37 = (f32[2048,128]{1,0:T(8,128)S(1)}, f32[64,128]{1,0:T(8,128)S(1)}) custom-call(s32[32]{0:T(128)} %shift_ref.1, f32[2048,128]{1,0:T(8,128)} %bitcast.3, f32[2048,128]{1,0:T(8,128)} %bitcast.4), custom_call_target="tpu_custom_call" | custom-call | tf_op jit(solution)/shard_map/pallas_call | solution.py:343
  13.3 1.1 %shard_map.38 = f32[2048,128]{1,0:T(8,128)} custom-call(f32[2048,128]{1,0:T(8,128)S(1)} %get-tuple-element.7.inside, f32[64,128]{1,0:T(8,128)S(1)} %get-tuple-element.8.side), custom_call_target="tpu_custom_call" | custom-call | tf_op jit(solution)/shard_map/pallas_call | solution.py:375

commit v5 on v4

--- a/solution.py
+++ b/solution.py
@@ -10,7 +10,7 @@
 SHEAR_V = 0.75
 SCALE = 0.05
 LANES = 128
-FIRST = 16
+FIRST = 32
 ROWS = 8
 MESH = pl.DeviceIdType.MESH
 

time: 14.5 us -> 14.5 us (level)
  no operation moved by 1% of the time
where the time goes in v5:
time: 14.5 us; the launch traced here: 14.4 us
  Pallas kernels  14.4 us (99%)
    pallas_call x1, Pallas kernels, on_device(): pl.pallas_call(functools.partial(kernel, outer, inner, planes), out_shape...  13.3 us
    pallas_call x1, Pallas kernels, on_device(): pl.pallas_call(functools.partial(finish, planes), out_shape=jax.ShapeDtyp...  1.13 us

profile of v5, /device:TPU:0, one launch (start us, length us, event | category | flops | bytes accessed | tf_op | source)
XLA Modules:
  0.0 14.4 jit_solution(11803857281445446877)
XLA Ops:
  0.0 13.3 %shard_map.37 = (f32[2048,128]{1,0:T(8,128)S(1)}, f32[64,128]{1,0:T(8,128)S(1)}) custom-call(s32[32]{0:T(128)} %shift_ref.1, f32[2048,128]{1,0:T(8,128)} %bitcast.3, f32[2048,128]{1,0:T(8,128)} %bitcast.4), custom_call_target="tpu_custom_call" | custom-call | tf_op jit(solution)/shard_map/pallas_call | solution.py:343
  13.3 1.1 %shard_map.38 = f32[2048,128]{1,0:T(8,128)} custom-call(f32[2048,128]{1,0:T(8,128)S(1)} %get-tuple-element.7.inside, f32[64,128]{1,0:T(8,128)S(1)} %get-tuple-element.8.side), custom_call_target="tpu_custom_call" | custom-call | tf_op jit(solution)/shard_map/pallas_call | solution.py:375
